TPU v7x, 256 devices: a whole 4x4x8 slice. The times are simulated.
256 devices in a mesh: section: 4 (over y), shard: 64 (over z, x, core).
Axes of the slice: x: 4, y: 4, z: 8, core: 2. Of those that a mesh axis runs over, the one named last changes fastest.
Arguments:
- memory: bfloat16 [131072, 512], P('shard'), may hold values from -3 to 3
- last_time: int32 [131072], P('shard'), may hold values from 0 to 999
- requests: int32 [4, 64, 64, 1], P('section', 'shard'), may hold values from -1 to 255, as said below
- event_source: int32 [4, 16384], P('section', 'shard'), may hold values from 0 to 511, as said below
- event_target: int32 [4, 16384], P('section', 'shard'), may hold values from 0 to 511, as said below
- event_time: int32 [4, 16384], P('section', 'shard'), may hold values from 1000 to 4999, as said below
- neighbour_blocks: int32 [4, 16384, 4], P('section', 'shard'), may hold values from 0 to 63, as said below
- time_rates: float32 [128], replicated, may hold values from 0.001 to 1
- time_phase: float32 [128], replicated, may hold values from -3.140625 to 3.140625
- w_input: bfloat16 [1152, 1536], replicated, may hold values from -0.1875 to 0.1875
- w_hidden: bfloat16 [512, 1536], replicated, may hold values from -0.25 to 0.25
- bias_input: float32 [1536], replicated, may hold values from -3 to 3
- w_neighbour: bfloat16 [512, 512], replicated, may hold values from -0.25 to 0.25
Outputs:
- memory_after: bfloat16 [4, 131072, 512], P('section', 'shard')
- embeddings: bfloat16 [4, 16384, 512], P('section', 'shard')
Inputs may be any that keep to these rules, and one draw needn't show every extreme that they name: `requests`: entry [b, j, o, c] is a block number among owner o's 256 blocks, or -1 for an empty slot; within one batch b each block of an owner is listed at most once among all devices; slot [b, j, j, 0] is never empty. `event_source`: events of device j in batch b name rows of blocks of non-empty slots [b, j, o, c]. `event_target`: events of device j in batch b name rows of blocks of non-empty slots [b, j, o, c]. `event_time`: times of batch b lie in [1000 (b + 1), 1000 (b + 2)). `neighbour_blocks`: positions of non-empty slots requested by the same device in the same batch.
All inputs are finite; a program needn't handle non-finite values.
Results may differ from a plain program's by a relative error of at most 0.004.
Values may be sent and summed in bfloat16 or wider, within the bound.
No kernel may reach another device: no remote copies, remote signals or barrier semaphores. Data moves between devices by JAX's collectives and lax.ppermute only.
A program may use at most 64 MiB of HBM per device.

v0:
```python
import functools

import jax
import jax.numpy as jnp
from jax import lax
from jax.experimental import pallas as pl
from jax.experimental.pallas import tpu as pltpu
from jax.sharding import PartitionSpec as P

BR = 8
NS = 4
LANES = 128
SLOTS = 64
ROWS = SLOTS * BR
EV = 256
BLOCKS = 256
M = 512
PUT = NS * BR
GET = PUT + NS
BF = jnp.bfloat16
F32 = jnp.float32
I32 = jnp.int32
VMEM = pltpu.VMEM
SMEM = pltpu.SMEM
HBM = pltpu.HBM
NT = (((1,), (1,)), ((), ()))


def spec(space=VMEM):
    return pl.BlockSpec(memory_space=space)


def call(body, outs, ins, to=None, scratch=(), flops=0, moved=0, aliases=None, mib=16):
    return pl.pallas_call(
        body,
        out_shape=outs,
        in_specs=[spec(s) for s in ins],
        out_specs=jax.tree.map(lambda _: spec(), outs) if to is None else to,
        scratch_shapes=list(scratch),
        input_output_aliases=aliases or {},
        compiler_params=pltpu.CompilerParams(vmem_limit_bytes=mib * 1024 * 1024),
        cost_estimate=pl.CostEstimate(flops=flops, bytes_accessed=moved, transcendentals=0),
    )


def wide(rows, at):
    return jnp.concatenate([rows[at : at + 1, :], rows[at + 1 : at + 2, :]], axis=1)


def message_rows(rows):
    source, target, when = wide(rows, 0), wide(rows, 2), wide(rows, 4)
    return (
        jnp.concatenate([source, target], axis=1),
        jnp.concatenate([target, source], axis=1),
        jnp.concatenate([when, when], axis=1),
    )


def as_column(row):
    n = row.shape[1]
    eye = lax.broadcasted_iota(I32, (n, n), 0) == lax.broadcasted_iota(I32, (n, n), 1)
    return jnp.sum(jnp.where(eye, row, jnp.zeros_like(row)), axis=1, keepdims=True)


def prep_kernel(sec_ref, w_in_ref, w_hid_ref, bias_ref, both_out, hid_out, code_out, bias_out):
    def quarter(g):
        return pl.ds(pl.multiple_of(g * M + sec_ref[0] * LANES, LANES), LANES)

    for g in range(3):
        to = slice(g * LANES, (g + 1) * LANES)
        both_out[:, to] = w_in_ref[0 : 2 * M, quarter(g)]
        code_out[:, to] = w_in_ref[2 * M :, quarter(g)]
        bias_out[:, to] = bias_ref[:, quarter(g)]
    for g in range(2):
        hid_out[:, g * LANES : (g + 1) * LANES] = w_hid_ref[:, quarter(g)]
    both_out[0:M, 3 * LANES :] = w_hid_ref[:, quarter(2)]
    both_out[M:, 3 * LANES :] = jnp.zeros((M, LANES), BF)


def events_kernel(sec_ref, ev_ref, pay_ref):
    sec = sec_ref[0]
    block = lax.broadcasted_iota(I32, (SLOTS, 2 * EV), 0) * BR
    lane = lax.broadcasted_iota(I32, (SLOTS, LANES), 1)
    pay = jnp.zeros((SLOTS, LANES), I32)
    for b in range(NS):
        rows = ev_ref[lax.rem(b + NS - sec, NS)]
        to, _, when = message_rows(rows)
        place = to - block
        for r in range(BR):
            latest = jnp.max(jnp.where(place == r, when, 0), axis=1, keepdims=True)
            pay = jnp.where(lane == b * BR + r, latest, pay)
        asked = as_column(rows[6:7, 0:SLOTS])
        pay = jnp.where(lane == PUT + b, jnp.where(asked < 0, BLOCKS, asked), pay)
        pay = jnp.where(lane == GET + b, jnp.where(asked < 0, BLOCKS + 1, asked), pay)
    pay_ref[...] = pay


def owner_kernel(got_ref, last_ref, table_ref, out_ref, rows_ref, table_out, ids_ref, sem):
    got = got_ref[...]
    flipped = jnp.transpose(
        jnp.concatenate([got.astype(F32), jnp.zeros((LANES - SLOTS, LANES), F32)], axis=0)
    ).astype(I32)
    rows_ref[...] = flipped[PUT : PUT + 2 * NS, :]
    scalars = pltpu.make_async_copy(rows_ref, ids_ref, sem)
    scalars.start()
    table_out[:BLOCKS] = table_ref[...]
    table_out[BLOCKS:] = jnp.zeros((8, BR, LANES), BF)
    cand = BLOCKS + NS * SLOTS
    lane = lax.broadcasted_iota(I32, (SLOTS, cand), 1)
    group = lax.broadcasted_iota(I32, (SLOTS, LANES), 1) // BR
    ids_row = jnp.concatenate(
        [lax.broadcasted_iota(I32, (1, BLOCKS), 1)]
        + [flipped[PUT + b : PUT + b + 1, 0:SLOTS] for b in range(NS)],
        axis=1,
    )
    match = jnp.concatenate(
        [
            ((got[:, GET + b : GET + b + 1] == ids_row) & (lane < BLOCKS + SLOTS * b)).astype(F32)
            for b in range(NS)
        ],
        axis=0,
    ).astype(BF)
    base = jnp.concatenate(
        [jnp.zeros((BLOCKS, (NS - 1) * BR), I32), last_ref[...], jnp.zeros((BLOCKS, LANES - NS * BR), I32)],
        axis=1,
    )
    times = jnp.concatenate(
        [base] + [jnp.where(group == b, got, 0) for b in range(NS - 1)] + [jnp.zeros((SLOTS, LANES), I32)],
        axis=0,
    )
    high = jnp.dot(match, (times >> 6).astype(F32).astype(BF), preferred_element_type=F32)
    low = jnp.dot(match, (times & 63).astype(F32).astype(BF), preferred_element_type=F32)
    stamp = high * 64.0 + low
    stamp = jnp.maximum(stamp, pltpu.roll(stamp, LANES - 2 * BR, 1))
    stamp = jnp.maximum(stamp, pltpu.roll(stamp, LANES - BR, 1)).astype(I32)
    total = jnp.zeros((SLOTS, LANES), I32)
    for b in range(NS):
        part = stamp[b * SLOTS : (b + 1) * SLOTS]
        part = pltpu.roll(part, b * BR, 1) if b else part
        total = jnp.where(group == b, part, total)
    packed = (total >> 6) + pltpu.roll(total & 63, PUT, 1)
    spread = jnp.broadcast_to(packed.astype(F32)[:, None, :], (SLOTS, BR, LANES))
    out_ref[:, :, LANES : 2 * LANES] = spread.astype(BF)
    scalars.wait()
    for j in range(SLOTS):
        out_ref[j, :, 0:LANES] = table_out[ids_ref[NS, j]]


def swap_kernel(b, ids_ref, table_ref, back_ref, out_ref, table_out):
    table_out[...] = table_ref[...]
    for j in range(SLOTS):
        table_out[ids_ref[b, j]] = back_ref[j]
    for j in range(SLOTS):
        out_ref[j] = table_out[ids_ref[NS + b + 1, j]]


def cosine(x):
    turns = jnp.round(x * 0.15915494309189535)
    x = x - turns * 6.28125
    x = x - turns * 0.0019340515136718750
    x = x - turns * 1.255665914e-06
    y = x * x
    total = jnp.full_like(y, -1.1470745597729725e-11)
    for c in (
        2.0876756987868099e-09,
        -2.7557319223985893e-07,
        2.4801587301587302e-05,
        -1.3888888888888889e-03,
        4.1666666666666667e-02,
        -0.5,
        1.0,
    ):
        total = total * y + c
    return total


def code_kernel(
    b,
    sec_ref,
    ev_ref,
    stamp_ref,
    rate_ref,
    phase_ref,
    w_code_ref,
    bias_ref,
    out_ref,
    pair_ref,
    share_ref,
):
    rows = ev_ref[lax.rem(b + NS - sec_ref[0], NS)]
    to, other, when = message_rows(rows)
    lane = lax.broadcasted_iota(I32, (ROWS, LANES), 1)
    sub = lax.broadcasted_iota(I32, (ROWS, LANES), 0) & (BR - 1)
    stamps = stamp_ref[:, LANES : 2 * LANES].astype(F32)
    scale = jnp.where(lane == b * BR + sub, 64.0, jnp.where(lane == PUT + b * BR + sub, 1.0, 0.0))
    state_time = jnp.sum(stamps * scale, axis=1, keepdims=True)
    slot = lax.broadcasted_iota(I32, (ROWS, 2 * EV), 0)
    hit = slot == to
    before = jnp.sum(jnp.where(hit, state_time, 0.0), axis=0, keepdims=True)
    delta = when.astype(F32) - before
    code = cosine(as_column(rate_ref[...]) * delta + as_column(phase_ref[...]))
    high = code.astype(BF)
    low = (code - high.astype(F32)).astype(BF)
    hits = hit.astype(F32)
    counts = jnp.sum(hits, axis=1, keepdims=True)
    hits = hits.astype(BF)
    total = lax.dot_general(hits, high, NT, preferred_element_type=F32)
    total = total + lax.dot_general(hits, low, NT, preferred_element_type=F32)
    mean = (total / jnp.maximum(counts, 1.0)).astype(BF)
    out_ref[...] = jnp.dot(mean, w_code_ref[...], preferred_element_type=F32) + bias_ref[...]
    share_ref[...] = jnp.where(counts > 0.0, 1.0 / jnp.maximum(counts, 1.0), 0.0)
    partner = (slot == other).astype(F32).astype(BF)
    pair_ref[...] = lax.dot_general(hits, partner, NT, preferred_element_type=F32).astype(BF)


def cell_kernel(
    b,
    sec_ref,
    own_ref,
    one_ref,
    two_ref,
    three_ref,
    pair_ref,
    code_ref,
    share_ref,
    w_both_ref,
    w_hid_ref,
    *refs,
):
    new_ref, kept_ref, all_ref, sem = refs[-4:]
    sec = sec_ref[0]
    for k, part in enumerate((own_ref, one_ref, two_ref, three_ref)):
        at = pl.multiple_of(lax.rem(sec + k, NS) * LANES, LANES)
        all_ref[:, pl.ds(at, LANES)] = part[...]
    keep = pltpu.make_async_copy(all_ref.at[:, 0:M], kept_ref, sem)

    @pl.when(sec == b)
    def _():
        keep.start()

    share = share_ref[...]
    states = all_ref[:, 0:M]
    trail = jnp.dot(pair_ref[...], states, preferred_element_type=F32) * share
    all_ref[:, M:] = trail.astype(BF)
    both = jnp.dot(all_ref[...], w_both_ref[...], preferred_element_type=F32)
    carried = jnp.dot(states, w_hid_ref[...], preferred_element_type=F32)
    given = code_ref[...]
    gates = both[:, : 2 * LANES] + carried + given[:, : 2 * LANES]
    gates = 0.5 + 0.5 * jnp.tanh(0.5 * gates)
    reset, update = gates[:, :LANES], gates[:, LANES:]
    candidate = both[:, 2 * LANES : 3 * LANES] + given[:, 2 * LANES :]
    candidate = jnp.tanh(candidate + reset * both[:, 3 * LANES :])
    old = own_ref[...].astype(F32)
    new = (1.0 - update) * candidate + update * old
    new_ref[...] = jnp.where(share > 0.0, new, old).astype(BF)

    @pl.when(sec == b)
    def _():
        keep.wait()


def early_kernel(sec_ref, ids_ref, mem_ref, own_ref, one_ref, two_ref, three_ref, out_ref, full_ref, sem):
    sec = sec_ref[0]
    fill = pltpu.make_async_copy(mem_ref, full_ref.at[pl.ds(0, BLOCKS)], sem)
    fill.start()
    fill.wait()
    for b in range(NS - 1):

        @pl.when(sec >= b)
        def _():
            for k, part in enumerate((own_ref, one_ref, two_ref, three_ref)):
                to = pl.multiple_of(lax.rem(sec + k, NS) * LANES, LANES)
                for j in range(SLOTS):
                    full_ref[ids_ref[b, j], :, pl.ds(to, LANES)] = part[b, j]

    drain = pltpu.make_async_copy(full_ref.at[pl.ds(0, BLOCKS)], out_ref, sem)
    drain.start()
    drain.wait()


def late_kernel(sec_ref, ids_ref, zero_ref, one_ref, two_ref, own_ref, early_ref, out_ref, full_ref, sems):
    @pl.when(sec_ref[0] == NS - 1)
    def _():
        for k, part in enumerate((zero_ref, one_ref, two_ref, own_ref)):
            full_ref[:, :, k * LANES : (k + 1) * LANES] = part[...]

        def place(j):
            at = ids_ref[NS - 1, j]
            return at, pltpu.make_async_copy(
                full_ref.at[j], out_ref.at[jnp.minimum(at, BLOCKS - 1)], sems.at[j]
            )

        for j in range(SLOTS):
            at, copy = place(j)

            @pl.when(at < BLOCKS)
            def _():
                copy.start()

        for j in range(SLOTS):
            at, copy = place(j)

            @pl.when(at < BLOCKS)
            def _():
                copy.wait()


def embed_kernel(source_ref, near_ref, kept_ref, weight_ref, out_ref):
    slot = lax.broadcasted_iota(I32, (EV, ROWS), 1)
    block = slot >> 3
    picks = jnp.zeros((EV, ROWS), F32)
    for k in range(near_ref.shape[0]):
        picks = picks + jnp.where(block == as_column(near_ref[k : k + 1, :]), 1.0 / BR, 0.0)
    states = kept_ref[...]
    near = jnp.dot(picks.astype(BF), states, preferred_element_type=F32).astype(BF)
    mixed = jnp.dot(near, weight_ref[...], preferred_element_type=F32)
    own = (slot == as_column(source_ref[...])).astype(F32).astype(BF)
    out_ref[...] = (jnp.dot(own, states, preferred_element_type=F32) + mixed).astype(BF)


def from_sections(array):
    return [array] + [
        lax.ppermute(array, "section", [(i, (i - k) % NS) for i in range(NS)]) for k in range(1, NS)
    ]


def exchange(array):
    return lax.all_to_all(array, "shard", split_axis=0, concat_axis=0, tiled=True)


def on_device(
    memory,
    last_time,
    requests,
    event_source,
    event_target,
    event_time,
    neighbour_blocks,
    time_rates,
    time_phase,
    w_input,
    w_hidden,
    bias_input,
    w_neighbour,
):
    sec = lax.axis_index("section")
    sec_ref = sec.astype(I32).reshape(1)
    source = event_source[0]
    ints = jnp.concatenate(
        [
            source,
            event_target[0],
            event_time[0],
            requests.reshape(SLOTS),
            jnp.zeros((8 * LANES - 3 * EV - SLOTS,), I32),
        ]
    ).reshape(8, LANES)
    parts = from_sections(ints)
    table = lax.dynamic_slice_in_dim(memory, sec * LANES, LANES, axis=1)
    last = last_time.reshape(BLOCKS, BR)
    bias_row = bias_input.reshape(1, -1)
    parts, table, last, bias_row = lax.optimization_barrier((parts, table, last, bias_row))
    events = jnp.stack(parts)
    pay = call(
        events_kernel, jax.ShapeDtypeStruct((SLOTS, LANES), I32), (SMEM, VMEM), moved=10**6
    )(sec_ref, events)
    ids = exchange(pay.reshape(SLOTS, 1, LANES)).reshape(SLOTS, LANES)
    picked, ids, table = call(
        owner_kernel,
        (
            jax.ShapeDtypeStruct((SLOTS, BR, 2 * LANES), BF),
            jax.ShapeDtypeStruct((2 * NS, LANES), I32),
            jax.ShapeDtypeStruct((BLOCKS + 8, BR, LANES), BF),
        ),
        (VMEM, VMEM, VMEM),
        scratch=(pltpu.SMEM((2 * NS, LANES), I32), pltpu.SemaphoreType.DMA),
        moved=10**6,
    )(ids, last, table.reshape(BLOCKS, BR, LANES))
    stamps = kept = None
    backs = []
    for b in range(NS):
        pulled = exchange(picked).reshape(ROWS, -1)
        if b == 0:
            stamps = pulled
            pulled = pulled[:, :LANES]
            pulled, later = lax.optimization_barrier((pulled, sec_ref))
            w_both, w_hid, w_code, bias = call(
                prep_kernel,
                (
                    jax.ShapeDtypeStruct((2 * M, 4 * LANES), BF),
                    jax.ShapeDtypeStruct((M, 2 * LANES), BF),
                    jax.ShapeDtypeStruct((LANES, 3 * LANES), BF),
                    jax.ShapeDtypeStruct((1, 3 * LANES), F32),
                ),
                (SMEM, VMEM, VMEM, VMEM),
                moved=3 * 10**6,
            )(later, w_input, w_hidden, bias_row)
        if b == NS - 1:
            early = from_sections(jnp.stack(backs))
            pulled, early[1] = lax.optimization_barrier((pulled, early[1]))
        parts = from_sections(pulled)
        if b == NS - 1:
            full = jax.ShapeDtypeStruct((BLOCKS, BR, M), BF)
            final = call(
                early_kernel,
                full,
                (SMEM, SMEM, pl.ANY) + (VMEM,) * NS,
                to=spec(pl.ANY),
                scratch=(pltpu.VMEM((BLOCKS + 8, BR, M), BF), pltpu.SemaphoreType.DMA),
                moved=8 * 10**6,
            )(sec_ref, ids, memory.reshape(BLOCKS, BR, M), *early)
            parts, final = lax.optimization_barrier((parts, final))
        code, pairs, share = call(
            functools.partial(code_kernel, b),
            (
                jax.ShapeDtypeStruct((ROWS, 3 * LANES), F32),
                jax.ShapeDtypeStruct((ROWS, ROWS), BF),
                jax.ShapeDtypeStruct((ROWS, 1), F32),
            ),
            (SMEM,) + (VMEM,) * 6,
            flops=2 * ROWS**3,
            moved=10**6,
        )(
            sec_ref,
            events,
            stamps,
            time_rates.reshape(1, LANES),
            time_phase.reshape(1, LANES),
            w_code,
            bias,
        )
        updated, kept = call(
            functools.partial(cell_kernel, b),
            (jax.ShapeDtypeStruct((ROWS, LANES), BF), jax.ShapeDtypeStruct((ROWS, M), BF)),
            (SMEM,) + (VMEM,) * 9 + ((pl.ANY,) if b else ()),
            to=(spec(), spec(pl.ANY)),
            scratch=(pltpu.VMEM((ROWS, 2 * M), BF), pltpu.SemaphoreType.DMA),
            flops=2 * ROWS * M * (M + 9 * LANES),
            moved=4 * 10**6,
            aliases={10: 1} if b else None,
        )(sec_ref, *parts, pairs, code, share, w_both, w_hid, *([kept] if b else []))
        updated = updated.reshape(SLOTS, BR, LANES)
        if b == NS - 1:
            updated, near, source = lax.optimization_barrier(
                (updated, neighbour_blocks[0].T, source)
            )
        back = exchange(updated)
        if b < NS - 1:
            backs.append(back)
            block = jax.ShapeDtypeStruct((SLOTS, BR, LANES), BF)
            whole = (BLOCKS + 8, BR, LANES)
            if b < NS - 2:
                picked, table = call(
                    functools.partial(swap_kernel, b),
                    (block, jax.ShapeDtypeStruct(whole, BF)),
                    (SMEM, VMEM, VMEM),
                    moved=10**6,
                )(ids, table, back)
            else:
                picked = call(
                    functools.partial(swap_kernel, b),
                    block,
                    (SMEM, VMEM, VMEM),
                    scratch=(pltpu.VMEM(whole, BF),),
                    moved=10**6,
                )(ids, table, back)

    late = [lax.ppermute(back, "section", [(k, NS - 1)]) for k in range(NS - 1)]
    final = call(
        late_kernel,
        full,
        (SMEM, SMEM) + (VMEM,) * NS + (pl.ANY,),
        to=spec(pl.ANY),
        scratch=(pltpu.VMEM((SLOTS, BR, M), BF), pltpu.SemaphoreType.DMA((SLOTS,))),
        moved=10**6,
        aliases={6: 0},
    )(sec_ref, ids, *late, back, final)

    embedded = call(
        embed_kernel,
        jax.ShapeDtypeStruct((EV, M), BF),
        (VMEM,) * 4,
        flops=2 * EV * M * (2 * ROWS + M),
        moved=10**6,
    )(source.reshape(1, EV), near, kept, w_neighbour)
    return (final.reshape(1, BLOCKS * BR, M), embedded[None])


def solution(mesh):
    return jax.shard_map(
        on_device,
        mesh=mesh,
        in_specs=(
            P("shard", None),
            P("shard"),
            P("section", "shard", None, None),
            P("section", "shard"),
            P("section", "shard"),
            P("section", "shard"),
            P("section", "shard", None),
            P(),
            P(),
            P(),
            P(),
            P(),
            P(),
        ),
        out_specs=(P("section", "shard", None), P("section", "shard", None)),
        check_vma=False,
    )
```

profile of v0, /device:TPU:24, one launch (start us, length us, event | category | flops | bytes accessed | tf_op | source)
XLA Modules:
  0.0 230.9 jit_solution(668338539634518944)
XLA Ops:
  0.6 0.9 concatenate.3
  1.6 0.7 collective-permute-start
  2.3 2.7 %collective-permute-start.1 = (s32[8,128]{1,0:T(8,128)S(1)}, s32[8,128]{1,0:T(8,128)S(1)}, u32[]{:S(2)}, u32[]{:S(2)}) collective-permute-start(s32[8,128]{1,0:T(8,128)S(1)} %bitcast.75), channel_id=1, source_target_pairs={{0,128},{64,192},{128,0},{192,64},{1,129},{65,193},{129,1},{193,65... | collective-permute-start | bytes 12296 | tf_op jit(solution)/shard_map/ppermute | solution.py:323
  5.0 0.4 collective-permute-start.2
  5.4 1.1 constant_dynamic-slice_fusion
  6.5 0.8 reshape.76.last_ref
  7.3 0.7 reshape.77.bias_ref
  8.0 0.6 collective-permute-done.2
  8.6 1.0 shard_map.140
  9.6 20.8 %all_to_all.45 = s32[64,1,128]{2,1,0:T(1,128)S(1)} all-to-all(s32[64,1,128]{2,1,0:T(1,128)S(1)} %bitcast.61), channel_id=1, replica_groups=mesh['section'=4,'shard'=64] {'shard'}, dimensions={0} | all-to-all | bytes 65536 | tf_op jit(solution)/shard_map/all_to_all | solution.py:328
  30.4 1.2 shard_map.141
  31.6 16.8 %all_to_all.46 = bf16[64,8,256]{2,1,0:T(8,128)(2,1)S(1)} all-to-all(bf16[64,8,256]{2,1,0:T(8,128)(2,1)S(1)} %get-tuple-element.60), channel_id=1, replica_groups=mesh['section'=4,'shard'=64] {'shard'}, dimensions={0} | all-to-all | bytes 524288 | tf_op jit(solution)/shard_map/all_to_all | solution.py:328
  48.4 1.3 collective-permute-start.3
  49.7 2.4 %collective-permute-start.4 = (bf16[512,128]{1,0:T(8,128)(2,1)S(1)}, bf16[512,128]{1,0:T(8,128)(2,1)S(1)}, u32[]{:S(2)}, u32[]{:S(2)}) collective-permute-start(bf16[512,128]{1,0:T(8,128)(2,1)S(1)} %slice.4.own_ref), channel_id=1, source_target_pairs={{0,128},{64,192},{128,0},{192,64},{1,129},{65,193},{129,1},{193,65... | collective-permute-start | bytes 393224 | tf_op jit(solution)/shard_map/ppermute | solution.py:323
  52.2 1.3 collective-permute-start.5
  53.4 2.0 copy-done
  55.4 0.2 shard_map.142
  55.7 1.9 shard_map.143
  57.6 0.0 collective-permute-done.3.one_ref
  57.6 1.0 collective-permute-done.4.two_ref
  58.6 0.2 collective-permute-done.5.three_ref
  58.7 1.4 shard_map.144
  60.1 15.7 %all_to_all.47.back_ref = bf16[64,8,128]{2,1,0:T(8,128)(2,1)S(1)} all-to-all(bf16[64,8,128]{2,1,0:T(8,128)(2,1)S(1)} %bitcast.60), channel_id=1, replica_groups=mesh['section'=4,'shard'=64] {'shard'}, dimensions={0} | all-to-all | bytes 262144 | tf_op jit(solution)/shard_map/all_to_all | solution.py:328
  75.9 0.7 shard_map.145
  76.6 15.0 %all_to_all.48 = bf16[64,8,128]{2,1,0:T(8,128)(2,1)S(1)} all-to-all(bf16[64,8,128]{2,1,0:T(8,128)(2,1)S(1)} %get-tuple-element.73), channel_id=1, replica_groups=mesh['section'=4,'shard'=64] {'shard'}, dimensions={0} | all-to-all | bytes 262144 | tf_op jit(solution)/shard_map/all_to_all | solution.py:328
  91.6 1.7 collective-permute-start.6
  93.3 2.5 %collective-permute-start.7 = (bf16[512,128]{1,0:T(8,128)(2,1)S(1)}, bf16[512,128]{1,0:T(8,128)(2,1)S(1)}, u32[]{:S(2)}, u32[]{:S(2)}) collective-permute-start(bf16[512,128]{1,0:T(8,128)(2,1)S(1)} %bitcast.50), channel_id=1, source_target_pairs={{0,128},{64,192},{128,0},{192,64},{1,129},{65,193},{129,1},{193,65... | collective-permute-start | bytes 393224 | tf_op jit(solution)/shard_map/ppermute | solution.py:323
  95.8 0.7 collective-permute-start.8
  96.5 1.9 shard_map.146
  98.4 3.7 %collective-permute-done.7.two_ref = bf16[512,128]{1,0:T(8,128)(2,1)S(1)} collective-permute-done((bf16[512,128]{1,0:T(8,128)(2,1)S(1)}, bf16[512,128]{1,0:T(8,128)(2,1)S(1)}, u32[]{:S(2)}, u32[]{:S(2)}) %collective-permute-start.7) | collective-permute-done | bytes 131104 | tf_op jit(solution)/shard_map/ppermute | solution.py:323
  102.1 1.4 shard_map.147
  103.5 14.9 %all_to_all.49.back_ref = bf16[64,8,128]{2,1,0:T(8,128)(2,1)S(1)} all-to-all(bf16[64,8,128]{2,1,0:T(8,128)(2,1)S(1)} %bitcast.58), channel_id=1, replica_groups=mesh['section'=4,'shard'=64] {'shard'}, dimensions={0} | all-to-all | bytes 262144 | tf_op jit(solution)/shard_map/all_to_all | solution.py:328
  118.4 0.7 shard_map.148
  119.1 14.9 %all_to_all.50 = bf16[64,8,128]{2,1,0:T(8,128)(2,1)S(1)} all-to-all(bf16[64,8,128]{2,1,0:T(8,128)(2,1)S(1)} %get-tuple-element.80), channel_id=1, replica_groups=mesh['section'=4,'shard'=64] {'shard'}, dimensions={0} | all-to-all | bytes 262144 | tf_op jit(solution)/shard_map/all_to_all | solution.py:328
  134.1 1.3 collective-permute-start.9
  135.4 2.4 %collective-permute-start.10 = (bf16[512,128]{1,0:T(8,128)(2,1)S(1)}, bf16[512,128]{1,0:T(8,128)(2,1)S(1)}, u32[]{:S(2)}, u32[]{:S(2)}) collective-permute-start(bf16[512,128]{1,0:T(8,128)(2,1)S(1)} %bitcast.54), channel_id=1, source_target_pairs={{0,128},{64,192},{128,0},{192,64},{1,129},{65,193},{129,1},{193,65... | collective-permute-start | bytes 393224 | tf_op jit(solution)/shard_map/ppermute | solution.py:323
  137.8 0.9 collective-permute-start.11
  138.7 1.9 shard_map.149
  140.6 0.5 collective-permute-done.9.one_ref
  141.1 3.0 %collective-permute-done.10.two_ref = bf16[512,128]{1,0:T(8,128)(2,1)S(1)} collective-permute-done((bf16[512,128]{1,0:T(8,128)(2,1)S(1)}, bf16[512,128]{1,0:T(8,128)(2,1)S(1)}, u32[]{:S(2)}, u32[]{:S(2)}) %collective-permute-start.10) | collective-permute-done | bytes 131104 | tf_op jit(solution)/shard_map/ppermute | solution.py:323
  144.1 0.1 collective-permute-done.11.three_ref
  144.2 11.1 %shard_map.150 = (bf16[512,128]{1,0:T(8,128)(2,1)S(1)}, bf16[512,512]{1,0:T(8,128)(2,1)S(1)}) custom-call(s32[1]{0:T(128)} %bitcast.sec_ref, bf16[512,128]{1,0:T(8,128)(2,1)S(1)} %bitcast.56, bf16[512,128]{1,0:T(8,128)(2,1)S(1)} %collective-permute-done.9.one_ref, ...), custom_call_target="tpu_custom_call", output_to_operand_aliasing={{1}: (10, {})} | custom-call | flops 872415232 | bytes 4000000 | tf_op jit(solution)/shard_map/pallas_call | solution.py:432
  155.3 0.0 copy-start.1
  155.3 15.1 %all_to_all.51.back_ref = bf16[64,8,128]{2,1,0:T(8,128)(2,1)S(1)} all-to-all(bf16[64,8,128]{2,1,0:T(8,128)(2,1)S(1)} %bitcast.59), channel_id=1, replica_groups=mesh['section'=4,'shard'=64] {'shard'}, dimensions={0} | all-to-all | bytes 262144 | tf_op jit(solution)/shard_map/all_to_all | solution.py:328
  170.5 1.5 collective-permute-start.12
  172.0 2.7 %collective-permute-start.16 = (bf16[3,64,8,128]{3,2,1,0:T(8,128)(2,1)S(1)}, bf16[3,64,8,128]{3,2,1,0:T(8,128)(2,1)S(1)}, u32[]{:S(2)}, u32[]{:S(2)}) collective-permute-start(bf16[3,64,8,128]{3,2,1,0:T(8,128)(2,1)S(1)} %pad_maximum_fusion.own_ref), channel_id=1, source_target_pairs={{0,128},{64,192},{128,0},{192,64},{1,129},{65,193},{129,1},{193,65... | collective-permute-start | bytes 1179656 | tf_op jit(solution)/shard_map/ppermute | solution.py:323
  174.7 0.5 collective-permute-start.17
  175.2 0.7 shard_map.151
  175.9 14.9 %all_to_all.52 = bf16[64,8,128]{2,1,0:T(8,128)(2,1)S(1)} all-to-all(bf16[64,8,128]{2,1,0:T(8,128)(2,1)S(1)} %shard_map.151), channel_id=1, replica_groups=mesh['section'=4,'shard'=64] {'shard'}, dimensions={0} | all-to-all | bytes 262144 | tf_op jit(solution)/shard_map/all_to_all | solution.py:328
  190.8 1.5 collective-permute-start.13
  192.3 0.9 collective-permute-start.14
  193.2 1.8 collective-permute-start.15
  195.0 1.9 shard_map.153
  196.9 3.2 %shard_map.152.early_ref = bf16[256,8,512]{2,1,0:T(8,128)(2,1)} custom-call(s32[1]{0:T(128)} %bitcast.sec_ref, s32[8,128]{1,0:T(8,128)S(1)} %get-tuple-element.58.ids_ref, bf16[256,8,512]{2,1,0:T(8,128)(2,1)S(1)} %bitcast.35, bf16[3,64,8,128]{3,2,1,0:T(8,128)(2,1)S(1)} %pad_maximum_fusion.own_ref, ...), custom_call_target="tpu_custom_call" | custom-call | bytes 8000000 | tf_op jit(solution)/shard_map/pallas_call | solution.py:404
  200.1 0.2 collective-permute-done.13.one_ref
  200.3 0.6 collective-permute-done.15.three_ref
  200.9 1.5 shard_map.154
  202.4 14.9 %all_to_all.53.own_ref = bf16[64,8,128]{2,1,0:T(8,128)(2,1)S(1)} all-to-all(bf16[64,8,128]{2,1,0:T(8,128)(2,1)S(1)} %bitcast.57), channel_id=1, replica_groups=mesh['section'=4,'shard'=64] {'shard'}, dimensions={0} | all-to-all | bytes 262144 | tf_op jit(solution)/shard_map/all_to_all | solution.py:328
  217.3 1.3 collective-permute-start.18
  218.6 1.3 collective-permute-start.19
  219.9 1.3 collective-permute-start.20
  221.2 1.6 shard_map.156
  222.8 5.9 %collective-permute-done.18.zero_ref = bf16[64,8,128]{2,1,0:T(8,128)(2,1)S(1)} collective-permute-done((bf16[64,8,128]{2,1,0:T(8,128)(2,1)S(1)}, bf16[64,8,128]{2,1,0:T(8,128)(2,1)S(1)}, u32[]{:S(2)}, u32[]{:S(2)}) %collective-permute-start.18) | collective-permute-done | bytes 131104 | tf_op jit(solution)/shard_map/ppermute | solution.py:468
  228.7 2.0 shard_map.155
  (28 shorter events, 0.1 us)
Async XLA Ops:
  0.6 52.8 %copy-start.2 = (bf16[512,1536]{1,0:T(8,128)(2,1)S(1)}, bf16[512,1536]{1,0:T(8,128)(2,1)}, u32[]{:S(2)}) copy-start(bf16[512,1536]{1,0:T(8,128)(2,1)} %w_hid_ref.1) | copy-start | bytes 4718596
  1.6 6.5 %collective-permute-start = (s32[8,128]{1,0:T(8,128)S(1)}, s32[8,128]{1,0:T(8,128)S(1)}, u32[]{:S(2)}, u32[]{:S(2)}) collective-permute-start(s32[8,128]{1,0:T(8,128)S(1)} %bitcast.74), channel_id=1, source_target_pairs={{0,192},{64,0},{128,64},{192,128},{1,193},{65,1},{129,65},{193,129... | collective-permute-start | bytes 12296 | tf_op jit(solution)/shard_map/ppermute | solution.py:323
  2.3 5.7 %collective-permute-start.1 = (s32[8,128]{1,0:T(8,128)S(1)}, s32[8,128]{1,0:T(8,128)S(1)}, u32[]{:S(2)}, u32[]{:S(2)}) collective-permute-start(s32[8,128]{1,0:T(8,128)S(1)} %bitcast.75), channel_id=1, source_target_pairs={{0,128},{64,192},{128,0},{192,64},{1,129},{65,193},{129,1},{193,65... | collective-permute-start | bytes 12296 | tf_op jit(solution)/shard_map/ppermute | solution.py:323
  5.0 3.6 %collective-permute-start.2 = (s32[8,128]{1,0:T(8,128)S(1)}, s32[8,128]{1,0:T(8,128)S(1)}, u32[]{:S(2)}, u32[]{:S(2)}) collective-permute-start(s32[8,128]{1,0:T(8,128)S(1)} %bitcast.76), channel_id=1, source_target_pairs={{0,64},{64,128},{128,192},{192,0},{1,65},{65,129},{129,193},{193,1... | collective-permute-start | bytes 12296 | tf_op jit(solution)/shard_map/ppermute | solution.py:323
  48.4 7.3 %copy-start.6 = (f32[128]{0:T(128)S(1)}, f32[128]{0:T(128)}, u32[]{:S(2)}) copy-start(f32[128]{0:T(128)} %param.20) | copy-start | bytes 1540
  48.4 7.3 %copy-start.7 = (f32[128]{0:T(128)S(1)}, f32[128]{0:T(128)}, u32[]{:S(2)}) copy-start(f32[128]{0:T(128)} %param.21) | copy-start | bytes 1540
  48.4 9.1 %collective-permute-start.3 = (bf16[512,128]{1,0:T(8,128)(2,1)S(1)}, bf16[512,128]{1,0:T(8,128)(2,1)S(1)}, u32[]{:S(2)}, u32[]{:S(2)}) collective-permute-start(bf16[512,128]{1,0:T(8,128)(2,1)S(1)} %slice.4.own_ref), channel_id=1, source_target_pairs={{0,192},{64,0},{128,64},{192,128},{1,193},{65,1},{129,65},{193,129... | collective-permute-start | bytes 393224 | tf_op jit(solution)/shard_map/ppermute | solution.py:323
  49.7 8.9 %collective-permute-start.4 = (bf16[512,128]{1,0:T(8,128)(2,1)S(1)}, bf16[512,128]{1,0:T(8,128)(2,1)S(1)}, u32[]{:S(2)}, u32[]{:S(2)}) collective-permute-start(bf16[512,128]{1,0:T(8,128)(2,1)S(1)} %slice.4.own_ref), channel_id=1, source_target_pairs={{0,128},{64,192},{128,0},{192,64},{1,129},{65,193},{129,1},{193,65... | collective-permute-start | bytes 393224 | tf_op jit(solution)/shard_map/ppermute | solution.py:323
  52.2 6.6 %collective-permute-start.5 = (bf16[512,128]{1,0:T(8,128)(2,1)S(1)}, bf16[512,128]{1,0:T(8,128)(2,1)S(1)}, u32[]{:S(2)}, u32[]{:S(2)}) collective-permute-start(bf16[512,128]{1,0:T(8,128)(2,1)S(1)} %slice.4.own_ref), channel_id=1, source_target_pairs={{0,64},{64,128},{128,192},{192,0},{1,65},{65,129},{129,193},{193,1... | collective-permute-start | bytes 393224 | tf_op jit(solution)/shard_map/ppermute | solution.py:323
  53.4 2.0 copy-start
  91.6 6.8 %collective-permute-start.6 = (bf16[512,128]{1,0:T(8,128)(2,1)S(1)}, bf16[512,128]{1,0:T(8,128)(2,1)S(1)}, u32[]{:S(2)}, u32[]{:S(2)}) collective-permute-start(bf16[512,128]{1,0:T(8,128)(2,1)S(1)} %bitcast.49), channel_id=1, source_target_pairs={{0,192},{64,0},{128,64},{192,128},{1,193},{65,1},{129,65},{193,129... | collective-permute-start | bytes 393224 | tf_op jit(solution)/shard_map/ppermute | solution.py:323
  93.3 8.8 %collective-permute-start.7 = (bf16[512,128]{1,0:T(8,128)(2,1)S(1)}, bf16[512,128]{1,0:T(8,128)(2,1)S(1)}, u32[]{:S(2)}, u32[]{:S(2)}) collective-permute-start(bf16[512,128]{1,0:T(8,128)(2,1)S(1)} %bitcast.50), channel_id=1, source_target_pairs={{0,128},{64,192},{128,0},{192,64},{1,129},{65,193},{129,1},{193,65... | collective-permute-start | bytes 393224 | tf_op jit(solution)/shard_map/ppermute | solution.py:323
  95.8 6.3 %collective-permute-start.8 = (bf16[512,128]{1,0:T(8,128)(2,1)S(1)}, bf16[512,128]{1,0:T(8,128)(2,1)S(1)}, u32[]{:S(2)}, u32[]{:S(2)}) collective-permute-start(bf16[512,128]{1,0:T(8,128)(2,1)S(1)} %bitcast.51), channel_id=1, source_target_pairs={{0,64},{64,128},{128,192},{192,0},{1,65},{65,129},{129,193},{193,1... | collective-permute-start | bytes 393224 | tf_op jit(solution)/shard_map/ppermute | solution.py:323
  134.1 7.0 %collective-permute-start.9 = (bf16[512,128]{1,0:T(8,128)(2,1)S(1)}, bf16[512,128]{1,0:T(8,128)(2,1)S(1)}, u32[]{:S(2)}, u32[]{:S(2)}) collective-permute-start(bf16[512,128]{1,0:T(8,128)(2,1)S(1)} %bitcast.53), channel_id=1, source_target_pairs={{0,192},{64,0},{128,64},{192,128},{1,193},{65,1},{129,65},{193,129... | collective-permute-start | bytes 393224 | tf_op jit(solution)/shard_map/ppermute | solution.py:323
  135.4 8.7 %collective-permute-start.10 = (bf16[512,128]{1,0:T(8,128)(2,1)S(1)}, bf16[512,128]{1,0:T(8,128)(2,1)S(1)}, u32[]{:S(2)}, u32[]{:S(2)}) collective-permute-start(bf16[512,128]{1,0:T(8,128)(2,1)S(1)} %bitcast.54), channel_id=1, source_target_pairs={{0,128},{64,192},{128,0},{192,64},{1,129},{65,193},{129,1},{193,65... | collective-permute-start | bytes 393224 | tf_op jit(solution)/shard_map/ppermute | solution.py:323
  137.8 6.4 %collective-permute-start.11 = (bf16[512,128]{1,0:T(8,128)(2,1)S(1)}, bf16[512,128]{1,0:T(8,128)(2,1)S(1)}, u32[]{:S(2)}, u32[]{:S(2)}) collective-permute-start(bf16[512,128]{1,0:T(8,128)(2,1)S(1)} %bitcast.55), channel_id=1, source_target_pairs={{0,64},{64,128},{128,192},{192,0},{1,65},{65,129},{129,193},{193,1... | collective-permute-start | bytes 393224 | tf_op jit(solution)/shard_map/ppermute | solution.py:323
  155.3 41.6 %copy-start.1 = (bf16[2048,512]{1,0:T(8,128)(2,1)S(1)}, bf16[2048,512]{1,0:T(8,128)(2,1)}, u32[]{:S(2)}) copy-start(bf16[2048,512]{1,0:T(8,128)(2,1)} %param.13) | copy-start | bytes 6291460
  170.5 20.3 %collective-permute-start.12 = (bf16[3,64,8,128]{3,2,1,0:T(8,128)(2,1)S(1)}, bf16[3,64,8,128]{3,2,1,0:T(8,128)(2,1)S(1)}, u32[]{:S(2)}, u32[]{:S(2)}) collective-permute-start(bf16[3,64,8,128]{3,2,1,0:T(8,128)(2,1)S(1)} %pad_maximum_fusion.own_ref), channel_id=1, source_target_pairs={{0,192},{64,0},{128,64},{192,128},{1,193},{65,1},{129,65},{193,129... | collective-permute-start | bytes 1179656 | tf_op jit(solution)/shard_map/ppermute | solution.py:323
  172.0 24.9 %collective-permute-start.16 = (bf16[3,64,8,128]{3,2,1,0:T(8,128)(2,1)S(1)}, bf16[3,64,8,128]{3,2,1,0:T(8,128)(2,1)S(1)}, u32[]{:S(2)}, u32[]{:S(2)}) collective-permute-start(bf16[3,64,8,128]{3,2,1,0:T(8,128)(2,1)S(1)} %pad_maximum_fusion.own_ref), channel_id=1, source_target_pairs={{0,128},{64,192},{128,0},{192,64},{1,129},{65,193},{129,1},{193,65... | collective-permute-start | bytes 1179656 | tf_op jit(solution)/shard_map/ppermute | solution.py:323
  174.7 22.2 %collective-permute-start.17 = (bf16[3,64,8,128]{3,2,1,0:T(8,128)(2,1)S(1)}, bf16[3,64,8,128]{3,2,1,0:T(8,128)(2,1)S(1)}, u32[]{:S(2)}, u32[]{:S(2)}) collective-permute-start(bf16[3,64,8,128]{3,2,1,0:T(8,128)(2,1)S(1)} %pad_maximum_fusion.own_ref), channel_id=1, source_target_pairs={{0,64},{64,128},{128,192},{192,0},{1,65},{65,129},{129,193},{193,1... | collective-permute-start | bytes 1179656 | tf_op jit(solution)/shard_map/ppermute | solution.py:323
  190.8 9.5 %collective-permute-start.13 = (bf16[512,128]{1,0:T(8,128)(2,1)S(1)}, bf16[512,128]{1,0:T(8,128)(2,1)S(1)}, u32[]{:S(2)}, u32[]{:S(2)}) collective-permute-start(bf16[512,128]{1,0:T(8,128)(2,1)S(1)} %bitcast.45), channel_id=1, source_target_pairs={{0,192},{64,0},{128,64},{192,128},{1,193},{65,1},{129,65},{193,129... | collective-permute-start | bytes 393224 | tf_op jit(solution)/shard_map/ppermute | solution.py:323
  192.3 8.0 %collective-permute-start.14 = (bf16[512,128]{1,0:T(8,128)(2,1)S(1)}, bf16[512,128]{1,0:T(8,128)(2,1)S(1)}, u32[]{:S(2)}, u32[]{:S(2)}) collective-permute-start(bf16[512,128]{1,0:T(8,128)(2,1)S(1)} %bitcast.46), channel_id=1, source_target_pairs={{0,128},{64,192},{128,0},{192,64},{1,129},{65,193},{129,1},{193,65... | collective-permute-start | bytes 393224 | tf_op jit(solution)/shard_map/ppermute | solution.py:323
  193.2 7.7 %collective-permute-start.15 = (bf16[512,128]{1,0:T(8,128)(2,1)S(1)}, bf16[512,128]{1,0:T(8,128)(2,1)S(1)}, u32[]{:S(2)}, u32[]{:S(2)}) collective-permute-start(bf16[512,128]{1,0:T(8,128)(2,1)S(1)} %bitcast.47), channel_id=1, source_target_pairs={{0,64},{64,128},{128,192},{192,0},{1,65},{65,129},{129,193},{193,1... | collective-permute-start | bytes 393224 | tf_op jit(solution)/shard_map/ppermute | solution.py:323
  200.9 20.3 %copy-start.3 = (s32[1,256]{1,0:T(1,128)S(1)}, s32[1,256]{1,0:T(1,128)}, u32[]{:S(2)}) copy-start(s32[1,256]{1,0:T(1,128)} %param.16) | copy-start | bytes 3076
  200.9 20.3 %copy-start.4 = (bf16[512,512]{1,0:T(8,128)(2,1)S(1)}, bf16[512,512]{1,0:T(8,128)(2,1)}, u32[]{:S(2)}) copy-start(bf16[512,512]{1,0:T(8,128)(2,1)} %weight_ref.1) | copy-start | bytes 1572868
  200.9 20.3 %copy-start.5 = (s32[1,256,4]{1,2,0:T(4,128)S(1)}, s32[1,256,4]{1,2,0:T(4,128)}, u32[]{:S(2)}) copy-start(s32[1,256,4]{1,2,0:T(4,128)} %param.19) | copy-start | bytes 12292
  217.3 11.4 %collective-permute-start.18 = (bf16[64,8,128]{2,1,0:T(8,128)(2,1)S(1)}, bf16[64,8,128]{2,1,0:T(8,128)(2,1)S(1)}, u32[]{:S(2)}, u32[]{:S(2)}) collective-permute-start(bf16[64,8,128]{2,1,0:T(8,128)(2,1)S(1)} %all_to_all.53.own_ref), channel_id=1, source_target_pairs={{0,192},{1,193},{2,194},{3,195},{4,196},{5,197},{6,198},{7,199},{8... | collective-permute-start | bytes 393224 | tf_op jit(solution)/shard_map/ppermute | solution.py:468
  218.6 10.1 %collective-permute-start.19 = (bf16[64,8,128]{2,1,0:T(8,128)(2,1)S(1)}, bf16[64,8,128]{2,1,0:T(8,128)(2,1)S(1)}, u32[]{:S(2)}, u32[]{:S(2)}) collective-permute-start(bf16[64,8,128]{2,1,0:T(8,128)(2,1)S(1)} %all_to_all.53.own_ref), channel_id=1, source_target_pairs={{64,192},{65,193},{66,194},{67,195},{68,196},{69,197},{70,198},{71... | collective-permute-start | bytes 393224 | tf_op jit(solution)/shard_map/ppermute | solution.py:468
  219.9 8.8 %collective-permute-start.20 = (bf16[64,8,128]{2,1,0:T(8,128)(2,1)S(1)}, bf16[64,8,128]{2,1,0:T(8,128)(2,1)S(1)}, u32[]{:S(2)}, u32[]{:S(2)}) collective-permute-start(bf16[64,8,128]{2,1,0:T(8,128)(2,1)S(1)} %all_to_all.53.own_ref), channel_id=1, source_target_pairs={{128,192},{129,193},{130,194},{131,195},{132,196},{133,197},{134,1... | collective-permute-start | bytes 393224 | tf_op jit(solution)/shard_map/ppermute | solution.py:468
where the time goes:
time: 235 us; the launch traced here: 231 us
  blocking collectives  143 us (61%)
  Pallas kernels  34.3 us (15%)
  starting transfers between devices  31.2 us (13%)
  waiting for transfers between devices  15.6 us (7%)
  local copies, waits for them, and re-layouts  5.52 us (2%)
    all_to_all x9, blocking collectives, exchange(): lax.all_to_all(array, 'shard', split_axis=0, concat_axis=0, tiled=True)  143 us
    ppermute x18, starting transfers between devices, from_sections(): lax.ppermute(array, 'section', [(i, (i - k) % NS) for i in range(NS)])  27.3 us
    pallas_call x4, Pallas kernels, on_device(): call(functools.partial(cell_kernel, b), (jax.ShapeDtypeStruct((ROWS, LANE...  15.3 us
    ppermute x18, waiting for transfers between devices, from_sections(): lax.ppermute(array, 'section', [(i, (i - k) % NS) for i in range(NS)])  9.78 us
    pallas_call x4, Pallas kernels, on_device(): call(functools.partial(code_kernel, b), (jax.ShapeDtypeStruct((ROWS, 3 *...  7.5 us
    ppermute x3, waiting for transfers between devices, on_device(): late = [lax.ppermute(back, 'section', [(k, NS - 1)]) for k in range(NS - 1)]  5.86 us
  transfers between devices with their start and end apart: 21, of which 10 were waited for; matrix products, arithmetic and copies ran while one was open for 1% of the time, Pallas kernels for 6%

commit v1 on v0

--- a/solution.py
+++ b/solution.py
@@ -70,7 +70,7 @@
         to = slice(g * LANES, (g + 1) * LANES)
         both_out[:, to] = w_in_ref[0 : 2 * M, quarter(g)]
         code_out[:, to] = w_in_ref[2 * M :, quarter(g)]
-        bias_out[:, to] = bias_ref[:, quarter(g)]
+        bias_out[:, to] = bias_ref[pl.ds(g * NS + sec_ref[0], 1), :]
     for g in range(2):
         hid_out[:, g * LANES : (g + 1) * LANES] = w_hid_ref[:, quarter(g)]
     both_out[0:M, 3 * LANES :] = w_hid_ref[:, quarter(2)]
@@ -358,7 +358,7 @@
     parts = from_sections(ints)
     table = lax.dynamic_slice_in_dim(memory, sec * LANES, LANES, axis=1)
     last = last_time.reshape(BLOCKS, BR)
-    bias_row = bias_input.reshape(1, -1)
+    bias_row = bias_input.reshape(3 * NS, LANES)
     parts, table, last, bias_row = lax.optimization_barrier((parts, table, last, bias_row))
     events = jnp.stack(parts)
     pay = call(

time: 235 us -> 235 us (level)
  no operation moved by 1% of the time
where the time goes in v1:
time: 235 us; the launch traced here: 230 us
  blocking collectives  142 us (60%)
  Pallas kernels  34.4 us (15%)
  starting transfers between devices  30.5 us (13%)
  waiting for transfers between devices  17 us (7%)
  local copies, waits for them, and re-layouts  4.83 us (2%)
    all_to_all x9, blocking collectives, exchange(): lax.all_to_all(array, 'shard', split_axis=0, concat_axis=0, tiled=True)  142 us
    ppermute x18, starting transfers between devices, from_sections(): lax.ppermute(array, 'section', [(i, (i - k) % NS) for i in range(NS)])  26.6 us
    pallas_call x4, Pallas kernels, on_device(): call(functools.partial(cell_kernel, b), (jax.ShapeDtypeStruct((ROWS, LANE...  15.3 us
    ppermute x18, waiting for transfers between devices, from_sections(): lax.ppermute(array, 'section', [(i, (i - k) % NS) for i in range(NS)])  11.2 us
    pallas_call x4, Pallas kernels, on_device(): call(functools.partial(code_kernel, b), (jax.ShapeDtypeStruct((ROWS, 3 *...  7.5 us
    ppermute x3, waiting for transfers between devices, on_device(): late = [lax.ppermute(back, 'section', [(k, NS - 1)]) for k in range(NS - 1)]  5.87 us
  transfers between devices with their start and end apart: 21, of which 10 were waited for; matrix products, arithmetic and copies ran while one was open for 1% of the time, Pallas kernels for 6%

profile of v1, /device:TPU:24, one launch (start us, length us, event | category | flops | bytes accessed | tf_op | source)
XLA Modules:
  0.0 230.3 jit_solution(8013336832275640330)
XLA Ops:
  0.7 0.9 concatenate.3
  1.6 0.7 collective-permute-start
  2.3 2.7 %collective-permute-start.1 = (s32[8,128]{1,0:T(8,128)S(1)}, s32[8,128]{1,0:T(8,128)S(1)}, u32[]{:S(2)}, u32[]{:S(2)}) collective-permute-start(s32[8,128]{1,0:T(8,128)S(1)} %bitcast.77), channel_id=1, source_target_pairs={{0,128},{64,192},{128,0},{192,64},{1,129},{65,193},{129,1},{193,65... | collective-permute-start | bytes 12296 | tf_op jit(solution)/shard_map/ppermute | solution.py:323
  5.0 0.4 collective-permute-start.2
  5.4 1.1 constant_dynamic-slice_fusion
  6.5 0.8 reshape.76.last_ref
  7.3 0.0 collective-permute-done
  7.3 0.1 collective-permute-done.1
  7.4 1.2 collective-permute-done.2
  8.6 1.0 shard_map.140
  9.6 20.2 %all_to_all.45 = s32[64,1,128]{2,1,0:T(1,128)S(1)} all-to-all(s32[64,1,128]{2,1,0:T(1,128)S(1)} %bitcast.62), channel_id=1, replica_groups=mesh['section'=4,'shard'=64] {'shard'}, dimensions={0} | all-to-all | bytes 65536 | tf_op jit(solution)/shard_map/all_to_all | solution.py:328
  29.8 1.2 shard_map.141
  31.0 16.8 %all_to_all.46 = bf16[64,8,256]{2,1,0:T(8,128)(2,1)S(1)} all-to-all(bf16[64,8,256]{2,1,0:T(8,128)(2,1)S(1)} %get-tuple-element.60), channel_id=1, replica_groups=mesh['section'=4,'shard'=64] {'shard'}, dimensions={0} | all-to-all | bytes 524288 | tf_op jit(solution)/shard_map/all_to_all | solution.py:328
  47.8 1.9 collective-permute-start.3
  49.7 2.4 %collective-permute-start.4 = (bf16[512,128]{1,0:T(8,128)(2,1)S(1)}, bf16[512,128]{1,0:T(8,128)(2,1)S(1)}, u32[]{:S(2)}, u32[]{:S(2)}) collective-permute-start(bf16[512,128]{1,0:T(8,128)(2,1)S(1)} %slice.4.own_ref), channel_id=1, source_target_pairs={{0,128},{64,192},{128,0},{192,64},{1,129},{65,193},{129,1},{193,65... | collective-permute-start | bytes 393224 | tf_op jit(solution)/shard_map/ppermute | solution.py:323
  52.2 0.6 collective-permute-start.5
  52.8 2.0 copy-done
  54.8 0.2 shard_map.142
  55.0 1.9 shard_map.143
  56.9 1.7 collective-permute-done.4.two_ref
  58.6 0.0 collective-permute-done.5.three_ref
  58.6 1.4 shard_map.144
  60.0 15.7 %all_to_all.47.back_ref = bf16[64,8,128]{2,1,0:T(8,128)(2,1)S(1)} all-to-all(bf16[64,8,128]{2,1,0:T(8,128)(2,1)S(1)} %bitcast.61), channel_id=1, replica_groups=mesh['section'=4,'shard'=64] {'shard'}, dimensions={0} | all-to-all | bytes 262144 | tf_op jit(solution)/shard_map/all_to_all | solution.py:328
  75.7 0.7 shard_map.145
  76.5 15.0 %all_to_all.48 = bf16[64,8,128]{2,1,0:T(8,128)(2,1)S(1)} all-to-all(bf16[64,8,128]{2,1,0:T(8,128)(2,1)S(1)} %get-tuple-element.73), channel_id=1, replica_groups=mesh['section'=4,'shard'=64] {'shard'}, dimensions={0} | all-to-all | bytes 262144 | tf_op jit(solution)/shard_map/all_to_all | solution.py:328
  91.4 1.2 collective-permute-start.6
  92.6 2.5 %collective-permute-start.7 = (bf16[512,128]{1,0:T(8,128)(2,1)S(1)}, bf16[512,128]{1,0:T(8,128)(2,1)S(1)}, u32[]{:S(2)}, u32[]{:S(2)}) collective-permute-start(bf16[512,128]{1,0:T(8,128)(2,1)S(1)} %bitcast.51), channel_id=1, source_target_pairs={{0,128},{64,192},{128,0},{192,64},{1,129},{65,193},{129,1},{193,65... | collective-permute-start | bytes 393224 | tf_op jit(solution)/shard_map/ppermute | solution.py:323
  95.2 0.7 collective-permute-start.8
  95.9 1.9 shard_map.146
  97.8 0.8 collective-permute-done.6.one_ref
  98.5 2.9 %collective-permute-done.7.two_ref = bf16[512,128]{1,0:T(8,128)(2,1)S(1)} collective-permute-done((bf16[512,128]{1,0:T(8,128)(2,1)S(1)}, bf16[512,128]{1,0:T(8,128)(2,1)S(1)}, u32[]{:S(2)}, u32[]{:S(2)}) %collective-permute-start.7) | collective-permute-done | bytes 131104 | tf_op jit(solution)/shard_map/ppermute | solution.py:323
  101.5 0.1 collective-permute-done.8.three_ref
  101.6 1.4 shard_map.147
  102.9 14.9 %all_to_all.49.back_ref = bf16[64,8,128]{2,1,0:T(8,128)(2,1)S(1)} all-to-all(bf16[64,8,128]{2,1,0:T(8,128)(2,1)S(1)} %bitcast.59), channel_id=1, replica_groups=mesh['section'=4,'shard'=64] {'shard'}, dimensions={0} | all-to-all | bytes 262144 | tf_op jit(solution)/shard_map/all_to_all | solution.py:328
  117.9 0.7 shard_map.148
  118.6 14.9 %all_to_all.50 = bf16[64,8,128]{2,1,0:T(8,128)(2,1)S(1)} all-to-all(bf16[64,8,128]{2,1,0:T(8,128)(2,1)S(1)} %get-tuple-element.80), channel_id=1, replica_groups=mesh['section'=4,'shard'=64] {'shard'}, dimensions={0} | all-to-all | bytes 262144 | tf_op jit(solution)/shard_map/all_to_all | solution.py:328
  133.5 1.2 collective-permute-start.9
  134.7 2.9 %collective-permute-start.10 = (bf16[512,128]{1,0:T(8,128)(2,1)S(1)}, bf16[512,128]{1,0:T(8,128)(2,1)S(1)}, u32[]{:S(2)}, u32[]{:S(2)}) collective-permute-start(bf16[512,128]{1,0:T(8,128)(2,1)S(1)} %bitcast.55), channel_id=1, source_target_pairs={{0,128},{64,192},{128,0},{192,64},{1,129},{65,193},{129,1},{193,65... | collective-permute-start | bytes 393224 | tf_op jit(solution)/shard_map/ppermute | solution.py:323
  137.7 0.4 collective-permute-start.11
  138.0 1.9 shard_map.149
  139.9 0.3 collective-permute-done.9.one_ref
  140.3 3.7 %collective-permute-done.10.two_ref = bf16[512,128]{1,0:T(8,128)(2,1)S(1)} collective-permute-done((bf16[512,128]{1,0:T(8,128)(2,1)S(1)}, bf16[512,128]{1,0:T(8,128)(2,1)S(1)}, u32[]{:S(2)}, u32[]{:S(2)}) %collective-permute-start.10) | collective-permute-done | bytes 131104 | tf_op jit(solution)/shard_map/ppermute | solution.py:323
  144.0 11.1 %shard_map.150 = (bf16[512,128]{1,0:T(8,128)(2,1)S(1)}, bf16[512,512]{1,0:T(8,128)(2,1)S(1)}) custom-call(s32[1]{0:T(128)} %bitcast.sec_ref, bf16[512,128]{1,0:T(8,128)(2,1)S(1)} %bitcast.57, bf16[512,128]{1,0:T(8,128)(2,1)S(1)} %collective-permute-done.9.one_ref, ...), custom_call_target="tpu_custom_call", output_to_operand_aliasing={{1}: (10, {})} | custom-call | flops 872415232 | bytes 4000000 | tf_op jit(solution)/shard_map/pallas_call | solution.py:432
  155.1 0.0 copy-start.1
  155.1 15.1 %all_to_all.51.back_ref = bf16[64,8,128]{2,1,0:T(8,128)(2,1)S(1)} all-to-all(bf16[64,8,128]{2,1,0:T(8,128)(2,1)S(1)} %bitcast.60), channel_id=1, replica_groups=mesh['section'=4,'shard'=64] {'shard'}, dimensions={0} | all-to-all | bytes 262144 | tf_op jit(solution)/shard_map/all_to_all | solution.py:328
  170.3 1.1 collective-permute-start.12
  171.4 2.8 %collective-permute-start.16 = (bf16[3,64,8,128]{3,2,1,0:T(8,128)(2,1)S(1)}, bf16[3,64,8,128]{3,2,1,0:T(8,128)(2,1)S(1)}, u32[]{:S(2)}, u32[]{:S(2)}) collective-permute-start(bf16[3,64,8,128]{3,2,1,0:T(8,128)(2,1)S(1)} %pad_maximum_fusion.own_ref), channel_id=1, source_target_pairs={{0,128},{64,192},{128,0},{192,64},{1,129},{65,193},{129,1},{193,65... | collective-permute-start | bytes 1179656 | tf_op jit(solution)/shard_map/ppermute | solution.py:323
  174.1 0.4 collective-permute-start.17
  174.5 0.7 shard_map.151
  175.3 14.9 %all_to_all.52 = bf16[64,8,128]{2,1,0:T(8,128)(2,1)S(1)} all-to-all(bf16[64,8,128]{2,1,0:T(8,128)(2,1)S(1)} %shard_map.151), channel_id=1, replica_groups=mesh['section'=4,'shard'=64] {'shard'}, dimensions={0} | all-to-all | bytes 262144 | tf_op jit(solution)/shard_map/all_to_all | solution.py:328
  190.1 1.7 collective-permute-start.13
  191.8 0.7 collective-permute-start.14
  192.5 2.2 collective-permute-start.15
  194.8 1.9 shard_map.153
  196.7 3.2 %shard_map.152.early_ref = bf16[256,8,512]{2,1,0:T(8,128)(2,1)} custom-call(s32[1]{0:T(128)} %bitcast.sec_ref, s32[8,128]{1,0:T(8,128)S(1)} %get-tuple-element.58.ids_ref, bf16[256,8,512]{2,1,0:T(8,128)(2,1)S(1)} %bitcast.36, bf16[3,64,8,128]{3,2,1,0:T(8,128)(2,1)S(1)} %pad_maximum_fusion.own_ref, ...), custom_call_target="tpu_custom_call" | custom-call | bytes 8000000 | tf_op jit(solution)/shard_map/pallas_call | solution.py:404
  199.9 0.4 collective-permute-done.15.three_ref
  200.3 1.5 shard_map.154
  201.7 14.9 %all_to_all.53.own_ref = bf16[64,8,128]{2,1,0:T(8,128)(2,1)S(1)} all-to-all(bf16[64,8,128]{2,1,0:T(8,128)(2,1)S(1)} %bitcast.58), channel_id=1, replica_groups=mesh['section'=4,'shard'=64] {'shard'}, dimensions={0} | all-to-all | bytes 262144 | tf_op jit(solution)/shard_map/all_to_all | solution.py:328
  216.6 1.3 collective-permute-start.18
  217.9 1.3 collective-permute-start.19
  219.2 1.3 collective-permute-start.20
  220.6 1.6 shard_map.156
  222.2 5.9 %collective-permute-done.18.zero_ref = bf16[64,8,128]{2,1,0:T(8,128)(2,1)S(1)} collective-permute-done((bf16[64,8,128]{2,1,0:T(8,128)(2,1)S(1)}, bf16[64,8,128]{2,1,0:T(8,128)(2,1)S(1)}, u32[]{:S(2)}, u32[]{:S(2)}) %collective-permute-start.18) | collective-permute-done | bytes 131104 | tf_op jit(solution)/shard_map/ppermute | solution.py:468
  228.1 2.0 shard_map.155
  (29 shorter events, 0.1 us)
Async XLA Ops:
  0.6 52.1 %copy-start.3 = (f32[1536]{0:T(1024)S(1)}, f32[1536]{0:T(1024)}, u32[]{:S(2)}) copy-start(f32[1536]{0:T(1024)} %param.24) | copy-start | bytes 18436
  0.6 52.1 %copy-start.2 = (bf16[512,1536]{1,0:T(8,128)(2,1)S(1)}, bf16[512,1536]{1,0:T(8,128)(2,1)}, u32[]{:S(2)}) copy-start(bf16[512,1536]{1,0:T(8,128)(2,1)} %w_hid_ref.1) | copy-start | bytes 4718596
  1.6 5.8 %collective-permute-start = (s32[8,128]{1,0:T(8,128)S(1)}, s32[8,128]{1,0:T(8,128)S(1)}, u32[]{:S(2)}, u32[]{:S(2)}) collective-permute-start(s32[8,128]{1,0:T(8,128)S(1)} %bitcast.76), channel_id=1, source_target_pairs={{0,192},{64,0},{128,64},{192,128},{1,193},{65,1},{129,65},{193,129... | collective-permute-start | bytes 12296 | tf_op jit(solution)/shard_map/ppermute | solution.py:323
  2.3 5.1 %collective-permute-start.1 = (s32[8,128]{1,0:T(8,128)S(1)}, s32[8,128]{1,0:T(8,128)S(1)}, u32[]{:S(2)}, u32[]{:S(2)}) collective-permute-start(s32[8,128]{1,0:T(8,128)S(1)} %bitcast.77), channel_id=1, source_target_pairs={{0,128},{64,192},{128,0},{192,64},{1,129},{65,193},{129,1},{193,65... | collective-permute-start | bytes 12296 | tf_op jit(solution)/shard_map/ppermute | solution.py:323
  5.0 3.6 %collective-permute-start.2 = (s32[8,128]{1,0:T(8,128)S(1)}, s32[8,128]{1,0:T(8,128)S(1)}, u32[]{:S(2)}, u32[]{:S(2)}) collective-permute-start(s32[8,128]{1,0:T(8,128)S(1)} %bitcast.78), channel_id=1, source_target_pairs={{0,64},{64,128},{128,192},{192,0},{1,65},{65,129},{129,193},{193,1... | collective-permute-start | bytes 12296 | tf_op jit(solution)/shard_map/ppermute | solution.py:323
  47.8 7.2 %copy-start.7 = (f32[128]{0:T(128)S(1)}, f32[128]{0:T(128)}, u32[]{:S(2)}) copy-start(f32[128]{0:T(128)} %param.20) | copy-start | bytes 1540
  47.8 7.2 %copy-start.8 = (f32[128]{0:T(128)S(1)}, f32[128]{0:T(128)}, u32[]{:S(2)}) copy-start(f32[128]{0:T(128)} %param.21) | copy-start | bytes 1540
  47.8 9.1 %collective-permute-start.3 = (bf16[512,128]{1,0:T(8,128)(2,1)S(1)}, bf16[512,128]{1,0:T(8,128)(2,1)S(1)}, u32[]{:S(2)}, u32[]{:S(2)}) collective-permute-start(bf16[512,128]{1,0:T(8,128)(2,1)S(1)} %slice.4.own_ref), channel_id=1, source_target_pairs={{0,192},{64,0},{128,64},{192,128},{1,193},{65,1},{129,65},{193,129... | collective-permute-start | bytes 393224 | tf_op jit(solution)/shard_map/ppermute | solution.py:323
  49.7 8.9 %collective-permute-start.4 = (bf16[512,128]{1,0:T(8,128)(2,1)S(1)}, bf16[512,128]{1,0:T(8,128)(2,1)S(1)}, u32[]{:S(2)}, u32[]{:S(2)}) collective-permute-start(bf16[512,128]{1,0:T(8,128)(2,1)S(1)} %slice.4.own_ref), channel_id=1, source_target_pairs={{0,128},{64,192},{128,0},{192,64},{1,129},{65,193},{129,1},{193,65... | collective-permute-start | bytes 393224 | tf_op jit(solution)/shard_map/ppermute | solution.py:323
  52.2 6.4 %collective-permute-start.5 = (bf16[512,128]{1,0:T(8,128)(2,1)S(1)}, bf16[512,128]{1,0:T(8,128)(2,1)S(1)}, u32[]{:S(2)}, u32[]{:S(2)}) collective-permute-start(bf16[512,128]{1,0:T(8,128)(2,1)S(1)} %slice.4.own_ref), channel_id=1, source_target_pairs={{0,64},{64,128},{128,192},{192,0},{1,65},{65,129},{129,193},{193,1... | collective-permute-start | bytes 393224 | tf_op jit(solution)/shard_map/ppermute | solution.py:323
  52.8 2.0 copy-start
  91.4 7.1 %collective-permute-start.6 = (bf16[512,128]{1,0:T(8,128)(2,1)S(1)}, bf16[512,128]{1,0:T(8,128)(2,1)S(1)}, u32[]{:S(2)}, u32[]{:S(2)}) collective-permute-start(bf16[512,128]{1,0:T(8,128)(2,1)S(1)} %bitcast.50), channel_id=1, source_target_pairs={{0,192},{64,0},{128,64},{192,128},{1,193},{65,1},{129,65},{193,129... | collective-permute-start | bytes 393224 | tf_op jit(solution)/shard_map/ppermute | solution.py:323
  92.6 8.8 %collective-permute-start.7 = (bf16[512,128]{1,0:T(8,128)(2,1)S(1)}, bf16[512,128]{1,0:T(8,128)(2,1)S(1)}, u32[]{:S(2)}, u32[]{:S(2)}) collective-permute-start(bf16[512,128]{1,0:T(8,128)(2,1)S(1)} %bitcast.51), channel_id=1, source_target_pairs={{0,128},{64,192},{128,0},{192,64},{1,129},{65,193},{129,1},{193,65... | collective-permute-start | bytes 393224 | tf_op jit(solution)/shard_map/ppermute | solution.py:323
  95.2 6.4 %collective-permute-start.8 = (bf16[512,128]{1,0:T(8,128)(2,1)S(1)}, bf16[512,128]{1,0:T(8,128)(2,1)S(1)}, u32[]{:S(2)}, u32[]{:S(2)}) collective-permute-start(bf16[512,128]{1,0:T(8,128)(2,1)S(1)} %bitcast.52), channel_id=1, source_target_pairs={{0,64},{64,128},{128,192},{192,0},{1,65},{65,129},{129,193},{193,1... | collective-permute-start | bytes 393224 | tf_op jit(solution)/shard_map/ppermute | solution.py:323
  133.5 6.7 %collective-permute-start.9 = (bf16[512,128]{1,0:T(8,128)(2,1)S(1)}, bf16[512,128]{1,0:T(8,128)(2,1)S(1)}, u32[]{:S(2)}, u32[]{:S(2)}) collective-permute-start(bf16[512,128]{1,0:T(8,128)(2,1)S(1)} %bitcast.54), channel_id=1, source_target_pairs={{0,192},{64,0},{128,64},{192,128},{1,193},{65,1},{129,65},{193,129... | collective-permute-start | bytes 393224 | tf_op jit(solution)/shard_map/ppermute | solution.py:323
  134.7 9.2 %collective-permute-start.10 = (bf16[512,128]{1,0:T(8,128)(2,1)S(1)}, bf16[512,128]{1,0:T(8,128)(2,1)S(1)}, u32[]{:S(2)}, u32[]{:S(2)}) collective-permute-start(bf16[512,128]{1,0:T(8,128)(2,1)S(1)} %bitcast.55), channel_id=1, source_target_pairs={{0,128},{64,192},{128,0},{192,64},{1,129},{65,193},{129,1},{193,65... | collective-permute-start | bytes 393224 | tf_op jit(solution)/shard_map/ppermute | solution.py:323
  137.7 6.3 %collective-permute-start.11 = (bf16[512,128]{1,0:T(8,128)(2,1)S(1)}, bf16[512,128]{1,0:T(8,128)(2,1)S(1)}, u32[]{:S(2)}, u32[]{:S(2)}) collective-permute-start(bf16[512,128]{1,0:T(8,128)(2,1)S(1)} %bitcast.56), channel_id=1, source_target_pairs={{0,64},{64,128},{128,192},{192,0},{1,65},{65,129},{129,193},{193,1... | collective-permute-start | bytes 393224 | tf_op jit(solution)/shard_map/ppermute | solution.py:323
  155.1 41.6 %copy-start.1 = (bf16[2048,512]{1,0:T(8,128)(2,1)S(1)}, bf16[2048,512]{1,0:T(8,128)(2,1)}, u32[]{:S(2)}) copy-start(bf16[2048,512]{1,0:T(8,128)(2,1)} %param.13) | copy-start | bytes 6291460
  170.3 19.9 %collective-permute-start.12 = (bf16[3,64,8,128]{3,2,1,0:T(8,128)(2,1)S(1)}, bf16[3,64,8,128]{3,2,1,0:T(8,128)(2,1)S(1)}, u32[]{:S(2)}, u32[]{:S(2)}) collective-permute-start(bf16[3,64,8,128]{3,2,1,0:T(8,128)(2,1)S(1)} %pad_maximum_fusion.own_ref), channel_id=1, source_target_pairs={{0,192},{64,0},{128,64},{192,128},{1,193},{65,1},{129,65},{193,129... | collective-permute-start | bytes 1179656 | tf_op jit(solution)/shard_map/ppermute | solution.py:323
  171.4 25.3 %collective-permute-start.16 = (bf16[3,64,8,128]{3,2,1,0:T(8,128)(2,1)S(1)}, bf16[3,64,8,128]{3,2,1,0:T(8,128)(2,1)S(1)}, u32[]{:S(2)}, u32[]{:S(2)}) collective-permute-start(bf16[3,64,8,128]{3,2,1,0:T(8,128)(2,1)S(1)} %pad_maximum_fusion.own_ref), channel_id=1, source_target_pairs={{0,128},{64,192},{128,0},{192,64},{1,129},{65,193},{129,1},{193,65... | collective-permute-start | bytes 1179656 | tf_op jit(solution)/shard_map/ppermute | solution.py:323
  174.1 22.5 %collective-permute-start.17 = (bf16[3,64,8,128]{3,2,1,0:T(8,128)(2,1)S(1)}, bf16[3,64,8,128]{3,2,1,0:T(8,128)(2,1)S(1)}, u32[]{:S(2)}, u32[]{:S(2)}) collective-permute-start(bf16[3,64,8,128]{3,2,1,0:T(8,128)(2,1)S(1)} %pad_maximum_fusion.own_ref), channel_id=1, source_target_pairs={{0,64},{64,128},{128,192},{192,0},{1,65},{65,129},{129,193},{193,1... | collective-permute-start | bytes 1179656 | tf_op jit(solution)/shard_map/ppermute | solution.py:323
  190.1 9.7 %collective-permute-start.13 = (bf16[512,128]{1,0:T(8,128)(2,1)S(1)}, bf16[512,128]{1,0:T(8,128)(2,1)S(1)}, u32[]{:S(2)}, u32[]{:S(2)}) collective-permute-start(bf16[512,128]{1,0:T(8,128)(2,1)S(1)} %bitcast.46), channel_id=1, source_target_pairs={{0,192},{64,0},{128,64},{192,128},{1,193},{65,1},{129,65},{193,129... | collective-permute-start | bytes 393224 | tf_op jit(solution)/shard_map/ppermute | solution.py:323
  191.8 8.1 %collective-permute-start.14 = (bf16[512,128]{1,0:T(8,128)(2,1)S(1)}, bf16[512,128]{1,0:T(8,128)(2,1)S(1)}, u32[]{:S(2)}, u32[]{:S(2)}) collective-permute-start(bf16[512,128]{1,0:T(8,128)(2,1)S(1)} %bitcast.47), channel_id=1, source_target_pairs={{0,128},{64,192},{128,0},{192,64},{1,129},{65,193},{129,1},{193,65... | collective-permute-start | bytes 393224 | tf_op jit(solution)/shard_map/ppermute | solution.py:323
  192.5 7.7 %collective-permute-start.15 = (bf16[512,128]{1,0:T(8,128)(2,1)S(1)}, bf16[512,128]{1,0:T(8,128)(2,1)S(1)}, u32[]{:S(2)}, u32[]{:S(2)}) collective-permute-start(bf16[512,128]{1,0:T(8,128)(2,1)S(1)} %bitcast.48), channel_id=1, source_target_pairs={{0,64},{64,128},{128,192},{192,0},{1,65},{65,129},{129,193},{193,1... | collective-permute-start | bytes 393224 | tf_op jit(solution)/shard_map/ppermute | solution.py:323
  200.3 20.3 %copy-start.4 = (s32[1,256]{1,0:T(1,128)S(1)}, s32[1,256]{1,0:T(1,128)}, u32[]{:S(2)}) copy-start(s32[1,256]{1,0:T(1,128)} %param.16) | copy-start | bytes 3076
  200.3 20.3 %copy-start.5 = (bf16[512,512]{1,0:T(8,128)(2,1)S(1)}, bf16[512,512]{1,0:T(8,128)(2,1)}, u32[]{:S(2)}) copy-start(bf16[512,512]{1,0:T(8,128)(2,1)} %weight_ref.1) | copy-start | bytes 1572868
  200.3 20.3 %copy-start.6 = (s32[1,256,4]{1,2,0:T(4,128)S(1)}, s32[1,256,4]{1,2,0:T(4,128)}, u32[]{:S(2)}) copy-start(s32[1,256,4]{1,2,0:T(4,128)} %param.19) | copy-start | bytes 12292
  216.6 11.4 %collective-permute-start.18 = (bf16[64,8,128]{2,1,0:T(8,128)(2,1)S(1)}, bf16[64,8,128]{2,1,0:T(8,128)(2,1)S(1)}, u32[]{:S(2)}, u32[]{:S(2)}) collective-permute-start(bf16[64,8,128]{2,1,0:T(8,128)(2,1)S(1)} %all_to_all.53.own_ref), channel_id=1, source_target_pairs={{0,192},{1,193},{2,194},{3,195},{4,196},{5,197},{6,198},{7,199},{8... | collective-permute-start | bytes 393224 | tf_op jit(solution)/shard_map/ppermute | solution.py:468
  217.9 10.1 %collective-permute-start.19 = (bf16[64,8,128]{2,1,0:T(8,128)(2,1)S(1)}, bf16[64,8,128]{2,1,0:T(8,128)(2,1)S(1)}, u32[]{:S(2)}, u32[]{:S(2)}) collective-permute-start(bf16[64,8,128]{2,1,0:T(8,128)(2,1)S(1)} %all_to_all.53.own_ref), channel_id=1, source_target_pairs={{64,192},{65,193},{66,194},{67,195},{68,196},{69,197},{70,198},{71... | collective-permute-start | bytes 393224 | tf_op jit(solution)/shard_map/ppermute | solution.py:468
  219.2 8.8 %collective-permute-start.20 = (bf16[64,8,128]{2,1,0:T(8,128)(2,1)S(1)}, bf16[64,8,128]{2,1,0:T(8,128)(2,1)S(1)}, u32[]{:S(2)}, u32[]{:S(2)}) collective-permute-start(bf16[64,8,128]{2,1,0:T(8,128)(2,1)S(1)} %all_to_all.53.own_ref), channel_id=1, source_target_pairs={{128,192},{129,193},{130,194},{131,195},{132,196},{133,197},{134,1... | collective-permute-start | bytes 393224 | tf_op jit(solution)/shard_map/ppermute | solution.py:468
